TPU v7x, 512 devices: a whole 4x4x16 slice. The times are simulated.
512 devices in a mesh: ctx: 128 (over z, y_lo, x), ch: 4 (over y_hi, core).
Axes of the slice: x: 4, y: 4 (y_hi: 2, y_lo: 2; y = y_hi * 2 + y_lo), z: 16, core: 2. Of those that a mesh axis runs over, the one named last changes fastest.
Arguments:
- tokens: bfloat16 [16384, 4096], P('ctx'), may hold values from -1000 to 1000, as said below
- norm_gain: float32 [4096], replicated, may hold values from 0.1 to 1.9
- in_proj: bfloat16 [4096, 3, 2048], P('ctx', None, 'ch'), may hold values from -0.09375 to 0.09375
- short_taps: float32 [3, 3, 2048], P(None, None, 'ch'), may hold values from -3 to 3
- decay: float32 [16, 2048], P(None, 'ch'), may hold values from 0 to 1, as said below
- residue: float32 [16, 2048], P(None, 'ch'), may hold values from -1.5 to 1.5
- skip: float32 [2048], P('ch'), may hold values from -4 to 4
Outputs:
- mixed: bfloat16 [16384, 2048], P('ctx', 'ch')
Inputs may be any that keep to these rules, and one draw needn't show every extreme that they name: `tokens`: every entry is finite. `decay`: every rate is positive.
All inputs are finite; a program needn't handle non-finite values.
Results may differ from a plain program's by a relative error of at most 0.01295.
Values may be sent and summed in bfloat16 or wider, within the bound.
A program may use at most 128 MiB of HBM per device.

v0:
```python
import math
import jax
import jax.numpy as jnp
from jax import lax
from jax.sharding import PartitionSpec as P


def passed_along(value, axis, steps):
    count = lax.axis_size(axis)
    initial, last = (max(0, -steps), min(count, count - steps))
    return lax.ppermute(value, axis, [(source, source + steps) for source in range(initial, last)])


def shortened(array):
    return jax.tree.map(lambda a: a.astype(jnp.bfloat16) if a.dtype == jnp.float32 else a, array)


def phase_table(left_index, right_index, period):
    product = left_index[:, None] * right_index[None, :] % period
    product = jnp.where(product > period // 2, product - period, product)
    return product.astype(jnp.float32) * (2.0 * math.pi / period)


def contract_rows(matrix, values):
    return jnp.einsum("sr,krc->ksc", matrix, values, precision=lax.Precision.HIGHEST)


def first_forward(blocks, r_index, total_len):
    count = blocks.shape[0]
    freq_index = jnp.arange(2 * count, dtype=jnp.int32)
    phases = phase_table(freq_index, jnp.arange(count, dtype=jnp.int32), 2 * count)
    flat = blocks.reshape(count, -1)
    out_shape = (2 * count,) + blocks.shape[1:]
    real_part = jnp.dot(jnp.cos(phases), flat, precision=lax.Precision.HIGHEST).reshape(out_shape)
    imag_part = -jnp.dot(jnp.sin(phases), flat, precision=lax.Precision.HIGHEST).reshape(out_shape)
    twist = phase_table(freq_index, r_index, total_len)
    cosine = jnp.cos(twist)[:, :, None]
    sine = jnp.sin(twist)[:, :, None]
    return (real_part * cosine + imag_part * sine, imag_part * cosine - real_part * sine)


def second_forward(real_part, imag_part):
    length = real_part.shape[1]
    steps_index = jnp.arange(length, dtype=jnp.int32)
    phases = phase_table(steps_index, steps_index, length)
    cosine = jnp.cos(phases)
    sine = jnp.sin(phases)
    out_real = contract_rows(cosine, real_part) + contract_rows(sine, imag_part)
    out_imag = contract_rows(cosine, imag_part) - contract_rows(sine, real_part)
    return (out_real, out_imag)


def first_inverse(real_part, imag_part, freq_index, total_len):
    length = real_part.shape[1]
    steps_index = jnp.arange(length, dtype=jnp.int32)
    phases = phase_table(steps_index, steps_index, length)
    cosine = jnp.cos(phases)
    sine = jnp.sin(phases)
    mid_real = contract_rows(cosine, real_part) - contract_rows(sine, imag_part)
    mid_imag = contract_rows(cosine, imag_part) + contract_rows(sine, real_part)
    twist = phase_table(freq_index, steps_index, total_len)
    tw_cos = jnp.cos(twist)[:, :, None]
    tw_sin = jnp.sin(twist)[:, :, None]
    return (mid_real * tw_cos - mid_imag * tw_sin, mid_imag * tw_cos + mid_real * tw_sin)


def second_inverse(real_part, imag_part, total_len):
    doubled = real_part.shape[0]
    count = doubled // 2
    phases = phase_table(
        jnp.arange(count, dtype=jnp.int32), jnp.arange(doubled, dtype=jnp.int32), doubled
    )
    flat_real = real_part.reshape(doubled, -1)
    flat_imag = imag_part.reshape(doubled, -1)
    result = jnp.dot(jnp.cos(phases), flat_real, precision=lax.Precision.HIGHEST)
    result = result - jnp.dot(jnp.sin(phases), flat_imag, precision=lax.Precision.HIGHEST)
    return (result * (1.0 / total_len)).reshape((count,) + real_part.shape[1:])


def spectrum(freq_index, decay_cols, residue_cols, length, count, seq_len, total_len):
    freq = freq_index[:, None] + 2 * count * jnp.arange(length, dtype=jnp.int32)[None, :]
    symmetric = jnp.where(freq > total_len // 2, freq - total_len, freq)
    half_phase = symmetric.astype(jnp.float32) * (math.pi / total_len)
    half_sq = (jnp.sin(half_phase) ** 2)[:, :, None]
    full_sin = jnp.sin(2.0 * half_phase)[:, :, None]
    parity = (1 - 2 * (freq % 2)).astype(jnp.float32)[:, :, None]
    shape_out = (freq_index.shape[0], length, decay_cols.shape[1])

    def add_mode(mode, carried):
        acc_real, acc_imag = carried
        rate = decay_cols[mode]
        amplitude = residue_cols[mode] * jnp.sqrt(2.0 * rate)
        ratio = jnp.exp(-rate)
        gap_term = -jnp.expm1(-rate)
        tail_term = jnp.exp(-rate * seq_len)
        along = gap_term + 2.0 * ratio * half_sq
        across = ratio * full_sin
        denom = gap_term * gap_term + 4.0 * ratio * half_sq
        numer = amplitude * (1.0 - tail_term * parity) / denom
        return (acc_real + numer * along, acc_imag - numer * across)

    zeros_block = jnp.zeros(shape_out, jnp.float32)
    return lax.fori_loop(0, decay_cols.shape[0], add_mode, (zeros_block, zeros_block))


def local(tokens, norm_gain, in_proj, short_taps, decay, residue, skip):
    tok_rows = tokens.shape[0]
    channels = in_proj.shape[2]
    devices = lax.axis_size("ctx")
    position = lax.axis_index("ctx")
    as_float = tokens.astype(jnp.float32)
    mean_square = jnp.mean(as_float * as_float, axis=1, keepdims=True)
    normed = (as_float * lax.rsqrt(mean_square + 1e-06) * norm_gain).astype(jnp.bfloat16)
    weight_piece = lax.all_gather(in_proj, "ctx", axis=0, tiled=True)
    piece_rows = weight_piece.shape[0]
    flat_piece = weight_piece.reshape(piece_rows, 3 * channels)
    projected = jnp.dot(normed, flat_piece, preferred_element_type=jnp.float32)
    proj = projected.astype(jnp.bfloat16).reshape(tok_rows, 3, channels)
    tap_count = short_taps.shape[0]
    rim_rows = passed_along(proj[tok_rows - (tap_count - 1) :], "ctx", 1)
    extended = jnp.concatenate([rim_rows, proj], axis=0)
    feats = jnp.zeros((tok_rows, 3, channels), jnp.float32)
    for shift_by in range(tap_count):
        window = extended[tap_count - 1 - shift_by : tap_count - 1 - shift_by + tok_rows].astype(
            jnp.float32
        )
        feats = feats + short_taps[shift_by] * window
    drive = feats[:, 1, :] * feats[:, 2, :]
    seq_len = tok_rows * devices
    total_len = 2 * seq_len
    group_rows = tok_rows // devices
    regrouped = drive.reshape(devices, group_rows, channels)
    arrived = lax.all_to_all(
        regrouped.astype(jnp.bfloat16), "ctx", split_axis=0, concat_axis=0, tiled=True
    ).astype(regrouped.dtype)
    r_index = position * group_rows + jnp.arange(group_rows, dtype=jnp.int32)
    front_real, front_imag = first_forward(arrived, r_index, total_len)
    middle = lax.all_to_all(
        jnp.stack([front_real, front_imag]).astype(jnp.bfloat16),
        "ctx",
        split_axis=1,
        concat_axis=2,
        tiled=True,
    ).astype(jnp.float32)
    spec_real, spec_imag = second_forward(middle[0], middle[1])
    freq_index = 2 * position + jnp.arange(2, dtype=jnp.int32)
    filt_real, filt_imag = spectrum(
        freq_index, decay, residue, tok_rows, devices, seq_len, total_len
    )
    prod_real = spec_real * filt_real - spec_imag * filt_imag
    prod_imag = spec_real * filt_imag + spec_imag * filt_real
    back_real, back_imag = first_inverse(prod_real, prod_imag, freq_index, total_len)
    returned = lax.all_to_all(
        shortened(jnp.stack([back_real, back_imag])), "ctx", split_axis=2, concat_axis=1, tiled=True
    )
    local_conv = second_inverse(returned[0], returned[1], total_len)
    conv = (
        lax.all_to_all(shortened(local_conv), "ctx", split_axis=0, concat_axis=1, tiled=True)
        .astype(local_conv.dtype)
        .reshape(tok_rows, channels)
    )
    return (feats[:, 0, :] * (conv + skip * drive)).astype(jnp.bfloat16)


def solution(mesh):
    placed = (
        P("ctx", None),
        P(),
        P("ctx", None, "ch"),
        P(None, None, "ch"),
        P(None, "ch"),
        P(None, "ch"),
        P("ch"),
    )
    return jax.shard_map(
        local, mesh=mesh, in_specs=placed, out_specs=P("ctx", "ch"), check_vma=False
    )
```

profile of v0, /device:TPU:8, one launch (start us, length us, event | category | flops | bytes accessed | tf_op | source)
XLA Modules:
  0.0 810.4 jit_solution(1913601212873430210)
XLA Ops:
  6.5 0.7 all-gather.2.cloned.1.call-update
  7.3 1.5 fusion.13
  8.8 611.6 %all-gather.2.cloned.1.call-done = bf16[4096,3,512]{2,0,1:T(8,128)(2,1)} async-done(((bf16[32,3,512]{2,0,1:T(8,128)(2,1)}), bf16[4096,3,512]{2,0,1:T(8,128)(2,1)}) %all-gather.2.cloned.1.call-update) | async-done | bytes 12582928 | tf_op jit(solution)/shard_map/all_gather | solution.py:114
  620.4 17.0 %copy.55 = bf16[4096,3,512]{0,2,1:T(8,128)(2,1)} copy(bf16[4096,3,512]{2,0,1:T(8,128)(2,1)} %all-gather.2.cloned.1.call-done) | data formatting | bytes 25165824 | tf_op jit(solution)/shard_map/all_gather | solution.py:114
  637.4 8.9 %convolution_convert_fusion = bf16[128,1536]{1,0:T(8,128)(2,1)S(1)} fusion(bf16[4096,1536]{0,1:T(8,128)(2,1)} %bitcast.120, bf16[128,4096]{1,0:T(8,128)(2,1)S(1)} %copy-done, f32[4096]{0:T(1024)S(1)} %copy-done.2, f32[128]{0:T(128)S(1)} %add_rsqrt_fusion), kind=kOutput, calls=%fused_computation.30 | convolution fusion | flops 1612906496 | bytes 14041600 | tf_op jit(solution)/shard_map/dot_general | solution.py:117
  646.6 3.3 collective-permute-start
  650.2 10.0 %collective-permute-done = bf16[2,3,512]{0,2,1:T(8,128)(2,1)S(1)} collective-permute-done((bf16[2,3,512]{0,2,1:T(8,128)(2,1)S(1)}, bf16[2,3,512]{0,2,1:T(8,128)(2,1)S(1)}, u32[]{:S(2)}, u32[]{:S(2)}) %collective-permute-start) | collective-permute-done | bytes 6176 | tf_op jit(solution)/shard_map/ppermute | solution.py:11
  660.2 1.1 multiply_add_fusion
  661.3 0.6 broadcast.788
  661.9 0.7 reduce
  662.6 0.7 reshape.468
  663.3 16.9 %all-to-all-start = ((bf16[128,2,256]{2,1,0:T(2,128)(2,1)}), bf16[128,2,256]{2,1,0:T(2,128)(2,1)S(1)}, u32[]{:S(2)}, u32[]{:S(2)}) async-start(bf16[128,2,256]{2,1,0:T(2,128)(2,1)} %reshape.468), calls=%async_computation | async-start | bytes 262144 | tf_op jit(solution)/shard_map/all_to_all | solution.py:133
  680.3 16.6 %all-to-all-done = bf16[128,2,256]{2,1,0:T(2,128)(2,1)S(1)} async-done(((bf16[128,2,256]{2,1,0:T(2,128)(2,1)}), bf16[128,2,256]{2,1,0:T(2,128)(2,1)S(1)}, u32[]{:S(2)}, u32[]{:S(2)}) %all-to-all-start) | async-done | bytes 131104 | tf_op jit(solution)/shard_map/all_to_all | solution.py:133
  697.0 0.8 convolution_negate_fusion
  697.9 0.9 fusion.25
  698.8 1.3 copy.59
  700.2 5.8 all-to-all-start.1
  705.9 22.7 %while.18 = (s32[]{:T(128)}, f32[2,128,512]{2,1,0:T(8,128)S(1)}, f32[2,128,512]{2,1,0:T(8,128)S(1)}, f32[16,512]{1,0:T(8,128)}, f32[16,512]{1,0:T(8,128)}, /*ind...) while((s32[]{:T(128)}, f32[2,128,512]{2,1,0:T(8,128)S(1)}, ...), condition=%wide.region_2.3_spmd.clone.clone.clone, body=%wide.region_1.2_spmd.clone.clone.clone.sunk | while | flops 1976067 | bytes 2139267 | solution.py:103
  706.1 0.8 sqrt_multiply_fusion.2
  706.9 0.4 select_subtract_fusion.2
  707.5 0.8 sqrt_multiply_fusion.2
  708.3 0.4 select_subtract_fusion.2
  708.9 0.8 sqrt_multiply_fusion.2
  709.8 0.4 select_subtract_fusion.2
  710.3 0.8 sqrt_multiply_fusion.2
  711.2 0.4 select_subtract_fusion.2
  711.7 0.8 sqrt_multiply_fusion.2
  712.6 0.4 select_subtract_fusion.2
  713.2 0.8 sqrt_multiply_fusion.2
  714.0 0.4 select_subtract_fusion.2
  714.6 0.8 sqrt_multiply_fusion.2
  715.4 0.4 select_subtract_fusion.2
  716.0 0.8 sqrt_multiply_fusion.2
  716.9 0.4 select_subtract_fusion.2
  717.4 0.8 sqrt_multiply_fusion.2
  718.3 0.4 select_subtract_fusion.2
  718.8 0.8 sqrt_multiply_fusion.2
  719.7 0.4 select_subtract_fusion.2
  720.3 0.8 sqrt_multiply_fusion.2
  721.1 0.4 select_subtract_fusion.2
  721.7 0.8 sqrt_multiply_fusion.2
  722.5 0.4 select_subtract_fusion.2
  723.1 0.8 sqrt_multiply_fusion.2
  724.0 0.4 select_subtract_fusion.2
  724.5 0.8 sqrt_multiply_fusion.2
  725.4 0.4 select_subtract_fusion.2
  725.9 0.8 sqrt_multiply_fusion.2
  727.4 0.8 sqrt_multiply_fusion.2
  729.5 0.5 copy.60
  730.1 0.6 fusion.31
  730.7 0.6 fusion.32
  731.3 0.6 fusion.17
  732.0 0.7 multiply_add_fusion.1
  732.7 0.8 fusion.61
  733.5 0.8 fusion.63
  734.3 0.8 convolution_add_fusion
  735.2 0.9 fusion.27
  736.2 0.5 copy.65
  736.7 40.1 %all_to_all.44 = bf16[2,2,128,512]{3,1,0,2:T(2,128)(2,1)S(1)} all-to-all(bf16[2,2,128,512]{3,1,0,2:T(2,128)(2,1)S(1)} %copy.65), channel_id=1, replica_groups=mesh['ctx'=128,'ch'=4] {'ctx'}, dimensions={2} | all-to-all | bytes 1048576 | tf_op jit(solution)/shard_map/all_to_all | solution.py:153
  777.3 0.8 fusion.47
  778.2 0.8 fusion.20
  779.0 0.7 reduce.1
  779.7 22.6 %all_to_all.45 = bf16[128,2,256]{2,1,0:T(2,128)(2,1)S(1)} all-to-all(bf16[128,2,256]{2,1,0:T(2,128)(2,1)S(1)} %reshape.470), channel_id=1, replica_groups=mesh['ctx'=128,'ch'=4] {'ctx'}, dimensions={0} | all-to-all | bytes 262144 | tf_op jit(solution)/shard_map/all_to_all | solution.py:158
  802.7 0.8 copy.68
  (85 shorter events, 7.0 us)
Async XLA Ops:
  6.5 613.9 %all-gather.2.cloned.1.call-start = ((), (), s32[]{:S(2)}) async-start(), calls=%async_computation.4 | async-start | bytes 12681216 | tf_op jit(solution)/shard_map/all_gather | solution.py:114
  8.8 628.6 %copy-start = (bf16[128,4096]{1,0:T(8,128)(2,1)S(1)}, bf16[128,4096]{1,0:T(8,128)(2,1)}, u32[]{:S(2)}) copy-start(bf16[128,4096]{1,0:T(8,128)(2,1)} %param.9) | copy-start | bytes 3145732
  8.8 628.6 %copy-start.2 = (f32[4096]{0:T(1024)S(1)}, f32[4096]{0:T(1024)}, u32[]{:S(2)}) copy-start(f32[4096]{0:T(1024)} %param.10) | copy-start | bytes 49156
  637.4 12.5 %copy-start.1 = (f32[3,3,512]{2,1,0:T(4,128)S(1)}, f32[3,3,512]{2,1,0:T(4,128)}, u32[]{:S(2)}) copy-start(f32[3,3,512]{2,1,0:T(4,128)} %param.12) | copy-start | bytes 55300
  646.6 13.6 %collective-permute-start = (bf16[2,3,512]{0,2,1:T(8,128)(2,1)S(1)}, bf16[2,3,512]{0,2,1:T(8,128)(2,1)S(1)}, u32[]{:S(2)}, u32[]{:S(2)}) collective-permute-start(bf16[2,3,512]{0,2,1:T(8,128)(2,1)S(1)} %bitcast.130), channel_id=1, source_target_pairs={{0,4},{4,8},{8,12},{12,16},{16,20},{20,24},{24,28},{28,32},{32,36}... | collective-permute-start | bytes 18440 | tf_op jit(solution)/shard_map/ppermute | solution.py:11
  663.3 33.6 %all-to-all-start = ((bf16[128,2,256]{2,1,0:T(2,128)(2,1)}), bf16[128,2,256]{2,1,0:T(2,128)(2,1)S(1)}, u32[]{:S(2)}, u32[]{:S(2)}) async-start(bf16[128,2,256]{2,1,0:T(2,128)(2,1)} %reshape.468), calls=%async_computation | async-start | bytes 262144 | tf_op jit(solution)/shard_map/all_to_all | solution.py:133
  700.2 29.4 %all-to-all-start.1 = ((bf16[2,256,1,512]{3,0,2,1:T(2,128)(2,1)}), bf16[2,256,1,512]{3,0,2,1:T(2,128)(2,1)S(1)}, u32[]{:S(2)}, u32[]{:S(2)}) async-start(bf16[2,256,1,512]{3,0,2,1:T(2,128)(2,1)} %copy.59), calls=%async_computation.1 | async-start | bytes 1048576 | tf_op jit(solution)/shard_map/all_to_all | solution.py:138
  777.2 25.4 %copy-start.3 = (f32[512]{0:T(512)S(1)}, f32[512]{0:T(512)}, u32[]{:S(2)}) copy-start(f32[512]{0:T(512)} %param.15) | copy-start | bytes 6148
Sparse Core Ops, SparseCore 0:
  9.4 610.8 all-gather.1
where the time goes:
time: 814 us; the launch traced here: 810 us
  waiting for transfers between devices  639 us (79%)
  blocking collectives  62.8 us (8%)
  other arithmetic  26.5 us (3%)
  starting transfers between devices  26 us (3%)
  local copies, waits for them, and re-layouts  23.4 us (3%)
  matrix products  18.1 us (2%)
  between operations  13.7 us (2%)
    all_gather x1, waiting for transfers between devices, local(): weight_piece = lax.all_gather(in_proj, 'ctx', axis=0, tiled=True)  612 us
    all_to_all x1, blocking collectives, local(): lax.all_to_all(shortened(jnp.stack([back_real, back_imag])), 'ctx', split...  40.1 us
    all_to_all x1, blocking collectives, local(): lax.all_to_all(shortened(local_conv), 'ctx', split_axis=0, concat_axis=1,...  22.6 us
    all_gather x1, local copies, waits for them, and re-layouts, local(): weight_piece = lax.all_gather(in_proj, 'ctx', axis=0, tiled=True)  17 us
    all_to_all x1, starting transfers between devices, local(): lax.all_to_all(regrouped.astype(jnp.bfloat16), 'ctx', split_axis=0, conca...  16.9 us
    all_to_all x1, waiting for transfers between devices, local(): lax.all_to_all(regrouped.astype(jnp.bfloat16), 'ctx', split_axis=0, conca...  16.6 us
  transfers between devices with their start and end apart: 4, of which 4 were waited for; matrix products, arithmetic and copies ran while one was open for 3% of the time, Pallas kernels for 0%

commit v1 on v0

--- a/solution.py
+++ b/solution.py
@@ -111,7 +111,15 @@
     as_float = tokens.astype(jnp.float32)
     mean_square = jnp.mean(as_float * as_float, axis=1, keepdims=True)
     normed = (as_float * lax.rsqrt(mean_square + 1e-06) * norm_gain).astype(jnp.bfloat16)
-    weight_piece = lax.all_gather(in_proj, "ctx", axis=0, tiled=True)
+    weight_piece = jnp.concatenate(
+        jax.lax.all_to_all(
+            jnp.stack(jax.lax.axis_size("ctx") * [in_proj], 0),
+            axis_name="ctx",
+            split_axis=0,
+            concat_axis=0,
+        ),
+        0,
+    )
     piece_rows = weight_piece.shape[0]
     flat_piece = weight_piece.reshape(piece_rows, 3 * channels)
     projected = jnp.dot(normed, flat_piece, preferred_element_type=jnp.float32)

time: 814 us -> 764 us (0.939)
  the two profiles are of different devices: /device:TPU:8 before, /device:TPU:24 now
where the time goes in v1:
time: 764 us; the launch traced here: 761 us
  waiting for transfers between devices  580 us (76%)
  blocking collectives  62.1 us (8%)
  starting transfers between devices  43.4 us (6%)
  local copies, waits for them, and re-layouts  37.7 us (5%)
  other arithmetic  25.1 us (3%)
  matrix products  11.2 us (1%)
    all_to_all x1, waiting for transfers between devices, local(): jax.lax.all_to_all(jnp.stack(jax.lax.axis_size('ctx') * [in_proj], 0), ax...  545 us
    all_to_all x1, blocking collectives, local(): lax.all_to_all(shortened(jnp.stack([back_real, back_imag])), 'ctx', split...  39.5 us
    all_to_all x1, blocking collectives, local(): lax.all_to_all(shortened(local_conv), 'ctx', split_axis=0, concat_axis=1,...  22.6 us
    all_to_all x1, starting transfers between devices, local(): jax.lax.all_to_all(jnp.stack(jax.lax.axis_size('ctx') * [in_proj], 0), ax...  20.9 us
    all_to_all x1, waiting for transfers between devices, local(): lax.all_to_all(regrouped.astype(jnp.bfloat16), 'ctx', split_axis=0, conca...  16.8 us
    all_to_all x1, local copies, waits for them, and re-layouts, local(): jax.lax.all_to_all(jnp.stack(jax.lax.axis_size('ctx') * [in_proj], 0), ax...  16.7 us
  transfers between devices with their start and end apart: 4, of which 4 were waited for; matrix products, arithmetic and copies ran while one was open for 3% of the time, Pallas kernels for 0%

profile of v1, /device:TPU:24, one launch (start us, length us, event | category | flops | bytes accessed | tf_op | source)
XLA Modules:
  0.0 760.7 jit_solution(9026255348213398489)
XLA Ops:
  0.0 7.0 stack.17
  7.0 20.9 %all-to-all-start = ((bf16[128,32,3,512]{3,1,2,0:T(8,128)(2,1)}), bf16[128,32,3,512]{3,1,2,0:T(8,128)(2,1)}, u32[]{:S(2)}, u32[]{:S(2)}) async-start(bf16[128,32,3,512]{3,1,2,0:T(8,128)(2,1)} %stack.17), calls=%async_computation | async-start | bytes 25165824 | tf_op jit(solution)/shard_map/all_to_all | solution.py:115
  28.2 544.8 %all-to-all-done = bf16[128,32,3,512]{3,1,2,0:T(8,128)(2,1)} async-done(((bf16[128,32,3,512]{3,1,2,0:T(8,128)(2,1)}), bf16[128,32,3,512]{3,1,2,0:T(8,128)(2,1)}, u32[]{:S(2)}, u32[]{:S(2)}) %all-to-all-start) | async-done | bytes 12582944 | tf_op jit(solution)/shard_map/all_to_all | solution.py:115
  573.0 16.7 %copy.56 = bf16[128,32,3,512]{3,2,1,0:T(4,128)(2,1)S(1)} copy(bf16[128,32,3,512]{3,1,2,0:T(8,128)(2,1)} %all-to-all-done) | data formatting | bytes 25165824 | tf_op jit(solution)/shard_map/all_to_all | solution.py:115
  589.8 7.6 %copy.72 = bf16[512,8,3,512]{3,1,2,0:T(8,128)(2,1)S(1)} copy(bf16[512,8,3,512]{3,2,1,0:T(4,128)(2,1)S(1)} %bitcast.123) | data formatting | bytes 25165824
  597.4 2.0 convolution_convert_fusion
  599.7 2.4 collective-permute-start
  602.4 9.1 %collective-permute-done = bf16[2,3,512]{0,2,1:T(8,128)(2,1)S(1)} collective-permute-done((bf16[2,3,512]{0,2,1:T(8,128)(2,1)S(1)}, bf16[2,3,512]{0,2,1:T(8,128)(2,1)S(1)}, u32[]{:S(2)}, u32[]{:S(2)}) %collective-permute-start) | collective-permute-done | bytes 6176 | tf_op jit(solution)/shard_map/ppermute | solution.py:11
  611.5 1.1 multiply_add_fusion
  612.6 0.5 broadcast.790
  613.1 0.6 reduce
  613.8 0.7 reshape.466
  614.5 14.1 %all-to-all-start.1 = ((bf16[128,2,256]{2,1,0:T(2,128)(2,1)}), bf16[128,2,256]{2,1,0:T(2,128)(2,1)S(1)}, u32[]{:S(2)}, u32[]{:S(2)}) async-start(bf16[128,2,256]{2,1,0:T(2,128)(2,1)} %reshape.466), calls=%async_computation.1 | async-start | bytes 262144 | tf_op jit(solution)/shard_map/all_to_all | solution.py:141
  628.7 16.8 %all-to-all-done.1 = bf16[128,2,256]{2,1,0:T(2,128)(2,1)S(1)} async-done(((bf16[128,2,256]{2,1,0:T(2,128)(2,1)}), bf16[128,2,256]{2,1,0:T(2,128)(2,1)S(1)}, u32[]{:S(2)}, u32[]{:S(2)}) %all-to-all-start.1) | async-done | bytes 131104 | tf_op jit(solution)/shard_map/all_to_all | solution.py:141
  645.6 0.8 convolution_negate_fusion
  646.4 0.9 fusion.25
  647.4 1.3 copy.60
  648.7 6.0 all-to-all-start.2
  654.7 22.7 %while.18 = (s32[]{:T(128)}, f32[2,128,512]{2,1,0:T(8,128)S(1)}, f32[2,128,512]{2,1,0:T(8,128)S(1)}, f32[16,512]{1,0:T(8,128)}, f32[16,512]{1,0:T(8,128)}, /*ind...) while((s32[]{:T(128)}, f32[2,128,512]{2,1,0:T(8,128)S(1)}, ...), condition=%wide.region_2.3_spmd.clone.clone.clone, body=%wide.region_1.2_spmd.clone.clone.clone.sunk | while | flops 1976067 | bytes 2139267 | solution.py:103
  654.8 0.8 sqrt_multiply_fusion.2
  655.7 0.4 select_subtract_fusion.2
  656.3 0.8 sqrt_multiply_fusion.2
  657.1 0.4 select_subtract_fusion.2
  657.7 0.8 sqrt_multiply_fusion.2
  658.5 0.4 select_subtract_fusion.2
  659.1 0.8 sqrt_multiply_fusion.2
  660.0 0.4 select_subtract_fusion.2
  660.5 0.8 sqrt_multiply_fusion.2
  661.4 0.4 select_subtract_fusion.2
  661.9 0.8 sqrt_multiply_fusion.2
  662.8 0.4 select_subtract_fusion.2
  663.4 0.8 sqrt_multiply_fusion.2
  664.2 0.4 select_subtract_fusion.2
  664.8 0.8 sqrt_multiply_fusion.2
  665.6 0.4 select_subtract_fusion.2
  666.2 0.8 sqrt_multiply_fusion.2
  667.1 0.4 select_subtract_fusion.2
  667.6 0.8 sqrt_multiply_fusion.2
  668.5 0.4 select_subtract_fusion.2
  669.0 0.8 sqrt_multiply_fusion.2
  669.9 0.4 select_subtract_fusion.2
  670.5 0.8 sqrt_multiply_fusion.2
  671.3 0.4 select_subtract_fusion.2
  671.9 0.8 sqrt_multiply_fusion.2
  673.3 0.8 sqrt_multiply_fusion.2
  674.7 0.8 sqrt_multiply_fusion.2
  676.1 0.8 sqrt_multiply_fusion.2
  678.0 9.5 %all-to-all-done.2 = bf16[2,256,1,512]{3,0,2,1:T(2,128)(2,1)S(1)} async-done(((bf16[2,256,1,512]{3,0,2,1:T(2,128)(2,1)}), bf16[2,256,1,512]{3,0,2,1:T(2,128)(2,1)S(1)}, u32[]{:S(2)}, u32[]{:S(2)}) %all-to-all-start.2) | async-done | bytes 524320 | tf_op jit(solution)/shard_map/all_to_all | solution.py:146
  687.5 0.5 copy.61
  688.0 0.6 fusion.31
  688.7 0.6 fusion.32
  689.3 0.6 fusion.17
  689.9 0.7 multiply_add_fusion.1
  690.6 0.8 fusion.61
  691.5 0.8 fusion.63
  692.3 0.8 convolution_add_fusion
  693.1 0.9 fusion.27
  694.1 0.5 copy.66
  694.6 39.5 %all_to_all.49 = bf16[2,2,128,512]{3,1,0,2:T(2,128)(2,1)S(1)} all-to-all(bf16[2,2,128,512]{3,1,0,2:T(2,128)(2,1)S(1)} %copy.66), channel_id=1, replica_groups=mesh['ctx'=128,'ch'=4] {'ctx'}, dimensions={2} | all-to-all | bytes 1048576 | tf_op jit(solution)/shard_map/all_to_all | solution.py:161
  734.6 0.8 fusion.47
  735.5 0.8 fusion.20
  736.2 0.6 reduce.1
  736.9 22.6 %all_to_all.50 = bf16[128,2,256]{2,1,0:T(2,128)(2,1)S(1)} all-to-all(bf16[128,2,256]{2,1,0:T(2,128)(2,1)S(1)} %reshape.468), channel_id=1, replica_groups=mesh['ctx'=128,'ch'=4] {'ctx'}, dimensions={0} | all-to-all | bytes 262144 | tf_op jit(solution)/shard_map/all_to_all | solution.py:166
  759.9 0.8 copy.69
  (86 shorter events, 7.7 us)
Async XLA Ops:
  7.0 20.9 %copy-start = (bf16[128,4096]{1,0:T(8,128)(2,1)S(1)}, bf16[128,4096]{1,0:T(8,128)(2,1)}, u32[]{:S(2)}) copy-start(bf16[128,4096]{1,0:T(8,128)(2,1)} %param.9) | copy-start | bytes 3145732
  7.0 566.0 %all-to-all-start = ((bf16[128,32,3,512]{3,1,2,0:T(8,128)(2,1)}), bf16[128,32,3,512]{3,1,2,0:T(8,128)(2,1)}, u32[]{:S(2)}, u32[]{:S(2)}) async-start(bf16[128,32,3,512]{3,1,2,0:T(8,128)(2,1)} %stack.17), calls=%async_computation | async-start | bytes 25165824 | tf_op jit(solution)/shard_map/all_to_all | solution.py:115
  589.7 7.7 %copy-start.1 = (f32[4096]{0:T(1024)S(1)}, f32[4096]{0:T(1024)}, u32[]{:S(2)}) copy-start(f32[4096]{0:T(1024)} %param.10) | copy-start | bytes 49156
  597.4 4.7 copy-start.2
  599.7 11.8 %collective-permute-start = (bf16[2,3,512]{0,2,1:T(8,128)(2,1)S(1)}, bf16[2,3,512]{0,2,1:T(8,128)(2,1)S(1)}, u32[]{:S(2)}, u32[]{:S(2)}) collective-permute-start(bf16[2,3,512]{0,2,1:T(8,128)(2,1)S(1)} %bitcast.133), channel_id=1, source_target_pairs={{0,4},{4,8},{8,12},{12,16},{16,20},{20,24},{24,28},{28,32},{32,36}... | collective-permute-start | bytes 18440 | tf_op jit(solution)/shard_map/ppermute | solution.py:11
  614.5 31.0 %all-to-all-start.1 = ((bf16[128,2,256]{2,1,0:T(2,128)(2,1)}), bf16[128,2,256]{2,1,0:T(2,128)(2,1)S(1)}, u32[]{:S(2)}, u32[]{:S(2)}) async-start(bf16[128,2,256]{2,1,0:T(2,128)(2,1)} %reshape.466), calls=%async_computation.1 | async-start | bytes 262144 | tf_op jit(solution)/shard_map/all_to_all | solution.py:141
  648.7 38.8 %all-to-all-start.2 = ((bf16[2,256,1,512]{3,0,2,1:T(2,128)(2,1)}), bf16[2,256,1,512]{3,0,2,1:T(2,128)(2,1)S(1)}, u32[]{:S(2)}, u32[]{:S(2)}) async-start(bf16[2,256,1,512]{3,0,2,1:T(2,128)(2,1)} %copy.60), calls=%async_computation.2 | async-start | bytes 1048576 | tf_op jit(solution)/shard_map/all_to_all | solution.py:146
  677.4 82.3 %copy-start.3 = (f32[512]{0:T(512)S(1)}, f32[512]{0:T(512)}, u32[]{:S(2)}) copy-start(f32[512]{0:T(512)} %param.15) | copy-start | bytes 6148
